TPU v7x, 32 devices: a whole 2x2x4 slice. The times are simulated.
32 devices in a mesh: shard: 4 (over y, x), context: 4 (over z), tensor: 2 (over core).
Axes of the slice: x: 2, y: 2, z: 4, core: 2. Of those that a mesh axis runs over, the one named last changes fastest.
Arguments:
- hidden_in: bfloat16 [4, 1024, 1024], P('shard', 'context'), may hold values from -6 to 6
- norm_gain: float32 [1024], replicated, may hold values from 0.5 to 1.5
- mamba_in: bfloat16 [1024, 2, 1536], P('shard', None, 'tensor'), may hold values from -0.1875 to 0.1875
- mamba_bc: bfloat16 [1024, 256], P('shard'), may hold values from -0.1875 to 0.1875
- mamba_dt: bfloat16 [1024, 24], P('shard', 'tensor'), may hold values from -0.1875 to 0.1875
- dt_bias: float32 [24], P('tensor'), may hold values from -1 to 0.5
- decay_seed: int32 [24], P('tensor'), may hold values from 0 to 9, as said below
- conv_x: float32 [4, 1536], P(None, 'tensor'), may hold values from -3 to 3
- conv_bc: float32 [4, 256], replicated, may hold values from -3 to 3
- skip_d: float32 [24], P('tensor'), may hold values from 0.5 to 2
- ssm_gain: float32 [1536], P('tensor'), may hold values from 0.5 to 1.5
- mamba_out: bfloat16 [1536, 1024], P('tensor', 'shard'), may hold values from -0.15625 to 0.15625
- attn_q: bfloat16 [1024, 512], P('shard', 'tensor'), may hold values from -0.1875 to 0.1875
- attn_kv: bfloat16 [1024, 2, 128], P('shard', None, 'tensor'), may hold values from -0.1875 to 0.1875
- attn_out: bfloat16 [512, 1024], P('tensor', 'shard'), may hold values from -1 to 1
- mlp_gain: float32 [1024], replicated, may hold values from 0.5 to 1.5
- mlp_gate_up: bfloat16 [1024, 2, 2048], P('shard', None, 'tensor'), may hold values from -0.1875 to 0.1875
- mlp_down: bfloat16 [2048, 1024], P('tensor', 'shard'), may hold values from -0.125 to 0.125
- cotangent: bfloat16 [4, 1024, 1024], P('shard', 'context'), may hold values from -6 to 6
Outputs:
- block_out: bfloat16 [4, 1024, 1024], P('shard', 'context')
- grad_input: bfloat16 [4, 1024, 1024], P('shard', 'context')
- grad_norm_gain: float32 [1024], replicated
- grad_mamba_in: float32 [1024, 2, 1536], P(('shard', 'context'), None, 'tensor')
- grad_mamba_bc: float32 [1024, 256], P(('shard', 'context'))
- grad_mamba_dt: float32 [1024, 24], P(('shard', 'context'), 'tensor')
- grad_dt_bias: float32 [24], P('tensor')
- grad_conv_x: float32 [4, 1536], P(None, 'tensor')
- grad_conv_bc: float32 [4, 256], replicated
- grad_skip_d: float32 [24], P('tensor')
- grad_ssm_gain: float32 [1536], P('tensor')
- grad_mamba_out: float32 [1536, 1024], P('tensor', ('shard', 'context'))
- grad_attn_q: float32 [1024, 512], P(('shard', 'context'), 'tensor')
- grad_attn_kv: float32 [1024, 2, 128], P(('shard', 'context'), None, 'tensor')
- grad_attn_out: float32 [512, 1024], P('tensor', ('shard', 'context'))
- grad_mlp_gain: float32 [1024], replicated
- grad_mlp_gate_up: float32 [1024, 2, 2048], P(('shard', 'context'), None, 'tensor')
- grad_mlp_down: float32 [2048, 1024], P('tensor', ('shard', 'context'))
Inputs may be any that keep to these rules, and one draw needn't show every extreme that they name: `decay_seed`: each head's decay seed is a whole number; with 10 or more heads every value from 0 to 9 occurs.
All inputs are finite; a program needn't handle non-finite values.
Results may differ from a plain program's by a relative error of at most 0.015.
The roundings to bfloat16 on the way count: a program that leaves them out, or rounds other values in their place, can miss the bound.
Values may be sent and summed in bfloat16 or wider, within the bound.
A program may use at most 128 MiB of HBM per device.

v0:
```python
from functools import partial

import jax
import jax.numpy as jnp
from jax import lax
from jax.sharding import PartitionSpec as P

D = 1024
HD = 64
STATE = 128
CONV = 4
DSSM = 1536


epsilon = 1e-05
rope_base = 100000000000.0


def passed_along(block, axis, distance):
    devices = range(lax.axis_size(axis))
    route = [(i - distance, i) for i in devices if i - distance in devices]
    return lax.ppermute(block, axis, route)


def entering(part, axis, combine, identity):
    place = lax.axis_index(axis)
    gathered = jax.tree.map(lambda a: lax.all_gather(a, axis), part)
    state = jax.tree.map(lambda a, e: jnp.zeros_like(a) + jnp.asarray(e, a.dtype), part, identity)

    def entering_one(step, state):
        return combine(
            state, jax.tree.map(lambda a: lax.dynamic_index_in_dim(a, step, 0, False), gathered)
        )

    return lax.fori_loop(0, place, entering_one, state)


def prefix(value, axis, join, neutral):
    count = lax.axis_size(axis)
    place = lax.axis_index(axis)
    ahead = count - 1 - place
    gathered = jax.tree.map(
        lambda a, kind: lax.all_gather(a.astype(kind), axis),
        value,
        jax.tree.map(lambda a: jnp.bfloat16 if a.dtype == jnp.float32 else a.dtype, value),
    )
    state = jax.tree.map(lambda a, e: jnp.zeros_like(a) + jnp.asarray(e, a.dtype), value, neutral)

    def prefix_one(step, state):
        source = count - 1 - step
        return join(
            state,
            jax.tree.map(
                lambda a, own: lax.dynamic_index_in_dim(a, source, 0, False).astype(own.dtype),
                gathered,
                value,
            ),
        )

    return lax.fori_loop(0, ahead, prefix_one, state)


def rms_scale(values, gain):
    return values * lax.rsqrt(jnp.mean(values * values, axis=-1, keepdims=True) + epsilon) * gain


def rotate(values, positions):
    half_dim = values.shape[-1] // 2
    frequency = rope_base ** (-2.0 * jnp.arange(half_dim, dtype=jnp.float32) / values.shape[-1])
    angles = positions[:, None] * frequency[None, :]
    cosine = jnp.cos(angles)[:, None, :]
    sine_part = jnp.sin(angles)[:, None, :]
    lower_half = values[..., :half_dim]
    upper_half = values[..., half_dim:]
    return jnp.concatenate(
        [
            lower_half * cosine - upper_half * sine_part,
            upper_half * cosine + lower_half * sine_part,
        ],
        axis=-1,
    )


def conv_silu(raw, history, weight):
    padded = jnp.concatenate([history, raw], axis=0)
    row_count = raw.shape[0]
    conv_sum = sum(
        (
            weight[kernel_step] * padded[kernel_step : kernel_step + row_count]
            for kernel_step in range(weight.shape[0])
        )
    )
    return jax.nn.silu(conv_sum)


def swiglu(gate_part, up_part):
    return jax.nn.silu(gate_part) * up_part


def section_one(raw_x, raw_bc, dt_raw, history, conv_x, conv_bc, dt_bias):
    x_width = raw_x.shape[1]
    x_conv = conv_silu(raw_x, history[:, :x_width], conv_x)
    bc_conv = conv_silu(raw_bc, history[:, x_width:], conv_bc)
    step_size = jax.nn.softplus(dt_raw + dt_bias)
    return (x_conv, bc_conv[:, :STATE], bc_conv[:, STATE:], step_size)


def section_two(x_conv, entry_map, read_map, step_size, skip_d, decay_rate):
    row_count = step_size.shape[0]
    head_count = step_size.shape[1]
    x_heads = x_conv.reshape(row_count, head_count, HD)
    log_decay = jnp.cumsum(step_size * decay_rate, axis=0)
    causal = jnp.arange(row_count)[:, None] >= jnp.arange(row_count)[None, :]
    gap_log = log_decay.T[:, :, None] - log_decay.T[:, None, :]
    decay_mask = jnp.where(causal, jnp.exp(jnp.where(causal, gap_log, 0.0)), 0.0)
    scores = jnp.dot(read_map, entry_map.T, precision=lax.Precision.HIGHEST)
    weighted = x_heads * step_size[:, :, None]
    inner_part = jnp.einsum(
        "hts,shp->thp", decay_mask * scores, weighted, precision=lax.Precision.HIGHEST
    )
    tail_weight = jnp.exp(log_decay[-1][None, :] - log_decay) * step_size
    local_state = jnp.einsum(
        "sh,shp,sn->hpn", tail_weight, x_heads, entry_map, precision=lax.Precision.HIGHEST
    )
    return (inner_part + skip_d[None, :, None] * x_heads, local_state, log_decay)


def section_three(y_local, state_in, read_map, log_decay, gate_z):
    carried = (
        jnp.einsum("tn,hpn->thp", read_map, state_in, precision=lax.Precision.HIGHEST)
        * jnp.exp(log_decay)[:, :, None]
    )
    ssm_out = (y_local + carried).reshape(y_local.shape[0], -1)
    return ssm_out * jax.nn.silu(gate_z)


def carry_forward(earlier, later):
    return (earlier[0] * later[0], later[0][:, None, None] * earlier[1] + later[1])


def carry_backward(earlier, later):
    return (later[0] * earlier[0], later[1] + later[0][:, None, None] * earlier[1])


def shards(
    hidden_in,
    norm_gain,
    mamba_in,
    mamba_bc,
    mamba_dt,
    dt_bias,
    decay_seed,
    conv_x,
    conv_bc,
    skip_d,
    ssm_gain,
    mamba_out,
    attn_q,
    attn_kv,
    attn_out,
    mlp_gain,
    mlp_gate_up,
    mlp_down,
    cotangent,
):
    in_full, bc_full, dt_full, mout_full, query_full, kv_full, attn_full, gu_full, down_full = (
        lax.all_gather(mamba_in, "shard", axis=0, tiled=True),
        lax.all_gather(mamba_bc, "shard", axis=0, tiled=True),
        lax.all_gather(mamba_dt, "shard", axis=0, tiled=True),
        lax.all_gather(mamba_out, "shard", axis=1, tiled=True),
        lax.all_gather(attn_q, "shard", axis=0, tiled=True),
        lax.all_gather(attn_kv, "shard", axis=0, tiled=True),
        lax.all_gather(attn_out, "shard", axis=1, tiled=True),
        lax.all_gather(mlp_gate_up, "shard", axis=0, tiled=True),
        lax.all_gather(mlp_down, "shard", axis=1, tiled=True),
    )
    row_in = hidden_in[0].astype(jnp.float32)
    tok_rows = row_in.shape[0]
    seq_len = tok_rows * lax.axis_size("context")
    positions_int = lax.axis_index("context") * tok_rows + jnp.arange(tok_rows, dtype=jnp.int32)
    positions = positions_int.astype(jnp.float32)
    score_scale = HD ** (-0.5)
    normed_f, pull_norm_one = jax.vjp(rms_scale, row_in, norm_gain)
    normed = normed_f.astype(jnp.bfloat16)
    x_width = in_full.shape[2]
    zx_proj = jnp.dot(
        normed, in_full.reshape(D, 2 * x_width), preferred_element_type=jnp.float32
    ).reshape(tok_rows, 2, x_width)
    bc_raw = jnp.dot(normed, bc_full, preferred_element_type=jnp.float32)
    dt_raw = jnp.dot(normed, dt_full, preferred_element_type=jnp.float32)
    raw_join = jnp.concatenate([zx_proj[:, 1], bc_raw], axis=1)
    history = passed_along(raw_join[tok_rows - (CONV - 1) :], "context", 1)
    decay_rate = -jnp.exp(0.5 * decay_seed.astype(jnp.float32)) / seq_len
    (x_conv, entry_map, read_map, step_size), pull_one = jax.vjp(
        section_one, zx_proj[:, 1], bc_raw, dt_raw, history, conv_x, conv_bc, dt_bias
    )
    (y_local, state_local, log_decay), pull_two = jax.vjp(
        partial(section_two, decay_rate=decay_rate), x_conv, entry_map, read_map, step_size, skip_d
    )
    block_decay = jnp.exp(log_decay[-1])
    unit_state = (
        jnp.ones(block_decay.shape, jnp.float32),
        jnp.zeros(state_local.shape, jnp.float32),
    )
    _, state_in = entering((block_decay, state_local), "context", carry_forward, unit_state)
    gated_y, pull_three = jax.vjp(
        section_three, y_local, state_in, read_map, log_decay, zx_proj[:, 0]
    )
    gated_b = (gated_y * ssm_gain).astype(jnp.bfloat16)
    mamba_part = jnp.dot(gated_b, mout_full, preferred_element_type=jnp.float32)
    square_part = jnp.sum(gated_y * gated_y, axis=-1)
    query_heads = query_full.shape[1] // HD
    kv_heads = kv_full.shape[2] // HD
    group_size = query_heads // kv_heads
    query_pre = jnp.dot(normed, query_full, preferred_element_type=jnp.float32).reshape(
        tok_rows, query_heads, HD
    )
    queries = (
        rotate(query_pre, positions)
        .astype(jnp.bfloat16)
        .reshape(tok_rows, kv_heads, group_size, HD)
    )
    kv_pre = jnp.dot(
        normed, kv_full.reshape(D, 2 * kv_heads * HD), preferred_element_type=jnp.float32
    ).reshape(tok_rows, 2, kv_heads, HD)
    keys_local = rotate(kv_pre[:, 0], positions).astype(jnp.bfloat16)
    values_local = kv_pre[:, 1].astype(jnp.bfloat16)
    kv_send = jnp.stack([keys_local, values_local], axis=1).reshape(tok_rows, 2 * kv_heads * HD)
    kv_every = lax.all_gather(kv_send, "context", axis=0, tiled=True).reshape(
        seq_len, 2, kv_heads, HD
    )
    keys_all = kv_every[:, 0]
    values_all = kv_every[:, 1]
    allowed = jnp.arange(seq_len, dtype=jnp.int32)[None, :] <= positions_int[:, None]

    def masked_scores():
        raw_scores = (
            jnp.einsum("tkgd,skd->kgts", queries, keys_all, preferred_element_type=jnp.float32)
            * score_scale
        )
        return jnp.where(allowed[None, None], raw_scores, -1e30)

    scores = masked_scores()
    log_total = jax.nn.logsumexp(scores, axis=-1, keepdims=True)
    probs_b = jnp.exp(scores - log_total).astype(jnp.bfloat16)
    attn_vals = jnp.einsum(
        "kgts,skd->tkgd", probs_b, values_all, preferred_element_type=jnp.float32
    )
    attn_vals = attn_vals.astype(jnp.bfloat16).reshape(tok_rows, query_heads * HD)
    attn_part = jnp.dot(attn_vals, attn_full, preferred_element_type=jnp.float32)
    attn_sum, mamba_sum, square_sum = lax.psum((attn_part, mamba_part, square_part), "tensor")
    ssm_scale = lax.rsqrt(square_sum / DSSM + epsilon)[:, None]
    resid = row_in + (attn_sum + ssm_scale * mamba_sum)
    normed_two_f, pull_norm_two = jax.vjp(rms_scale, resid, mlp_gain)
    normed_two = normed_two_f.astype(jnp.bfloat16)
    ff_local = gu_full.shape[2]
    gate_up = jnp.dot(
        normed_two, gu_full.reshape(D, 2 * ff_local), preferred_element_type=jnp.float32
    ).reshape(tok_rows, 2, ff_local)
    hidden_f, pull_gate = jax.vjp(swiglu, gate_up[:, 0], gate_up[:, 1])
    hidden = hidden_f.astype(jnp.bfloat16)
    down_part = jnp.dot(hidden, down_full, preferred_element_type=jnp.float32)
    out_grad = cotangent[0]
    grad_down = jnp.einsum("tf,td->fd", hidden, out_grad, preferred_element_type=jnp.float32)
    hidden_grad = jnp.einsum("td,fd->tf", out_grad, down_full, preferred_element_type=jnp.float32)
    gate_grad, up_grad = pull_gate(hidden_grad)
    gate_up_grad = jnp.stack([gate_grad, up_grad], axis=1).astype(jnp.bfloat16)
    grad_gate_up = jnp.einsum(
        "td,tjf->djf", normed_two, gate_up_grad, preferred_element_type=jnp.float32
    )
    normed_two_part = jnp.einsum(
        "tjf,djf->td", gate_up_grad, gu_full, preferred_element_type=jnp.float32
    )
    normed_two_grad = lax.psum(normed_two_part, "tensor")
    resid_norm_grad, grad_mlp_gain = pull_norm_two(normed_two_grad)
    resid_grad = out_grad.astype(jnp.float32) + resid_norm_grad
    mixed_grad = resid_grad.astype(jnp.bfloat16)
    grad_attn_o = jnp.einsum("th,td->hd", attn_vals, mixed_grad, preferred_element_type=jnp.float32)
    vals_grad = jnp.einsum("td,hd->th", mixed_grad, attn_full, preferred_element_type=jnp.float32)
    vals_grad = vals_grad.astype(jnp.bfloat16).reshape(tok_rows, kv_heads, group_size, HD)
    probs = jnp.exp(masked_scores() - log_total)
    probs_grad = jnp.einsum(
        "tkgd,skd->kgts", vals_grad, values_all, preferred_element_type=jnp.float32
    )
    score_grad = (
        probs * (probs_grad - jnp.sum(probs * probs_grad, axis=-1, keepdims=True))
    ).astype(jnp.bfloat16)
    query_grad = (
        jnp.einsum("kgts,skd->tkgd", score_grad, keys_all, preferred_element_type=jnp.float32)
        * score_scale
    )
    key_grad_all = (
        jnp.einsum("kgts,tkgd->skd", score_grad, queries, preferred_element_type=jnp.float32)
        * score_scale
    )
    value_grad_all = jnp.einsum(
        "kgts,tkgd->skd", probs.astype(jnp.bfloat16), vals_grad, preferred_element_type=jnp.float32
    )
    kv_grad_send = jnp.stack([key_grad_all, value_grad_all], axis=1).reshape(
        seq_len, 2 * kv_heads * HD
    )
    kv_grad = (
        lax.psum_scatter(
            kv_grad_send.astype(jnp.bfloat16), "context", scatter_dimension=0, tiled=True
        )
        .astype(jnp.float32)
        .reshape(tok_rows, 2, kv_heads, HD)
    )
    query_pre_grad = rotate(query_grad.reshape(tok_rows, query_heads, HD), -positions)
    query_pre_grad = query_pre_grad.reshape(tok_rows, query_heads * HD).astype(jnp.bfloat16)
    key_pre_grad = rotate(kv_grad[:, 0], -positions)
    kv_pre_grad = (
        jnp.stack([key_pre_grad, kv_grad[:, 1]], axis=1)
        .reshape(tok_rows, 2 * kv_heads * HD)
        .astype(jnp.bfloat16)
    )
    grad_query = jnp.einsum("td,th->dh", normed, query_pre_grad, preferred_element_type=jnp.float32)
    grad_kv = jnp.einsum(
        "td,th->dh", normed, kv_pre_grad, preferred_element_type=jnp.float32
    ).reshape(D, 2, kv_heads * HD)
    normed_grad = jnp.einsum(
        "th,dh->td", query_pre_grad, query_full, preferred_element_type=jnp.float32
    )
    normed_grad = normed_grad + jnp.einsum(
        "th,dh->td",
        kv_pre_grad,
        kv_full.reshape(D, 2 * kv_heads * HD),
        preferred_element_type=jnp.float32,
    )
    mixed_f = mixed_grad.astype(jnp.float32)
    scale_grad = jnp.sum(mixed_f * mamba_sum, axis=-1, keepdims=True)
    mamba_grad = (ssm_scale * mixed_f).astype(jnp.bfloat16)
    grad_mout = jnp.einsum("tc,td->cd", gated_b, mamba_grad, preferred_element_type=jnp.float32)
    gated_grad = jnp.einsum("td,cd->tc", mamba_grad, mout_full, preferred_element_type=jnp.float32)
    grad_ssm_gain = jnp.sum(gated_grad * gated_y, axis=0)
    y_grad = gated_grad * ssm_gain - scale_grad * ssm_scale * ssm_scale * ssm_scale * gated_y / DSSM
    y_local_grad, state_in_grad, read_grad_three, log_grad_three, gate_z_grad = pull_three(y_grad)
    _, state_out_grad = prefix((block_decay, state_in_grad), "context", carry_backward, unit_state)
    decay_grad = block_decay * jnp.sum(state_out_grad * state_in, axis=(1, 2))
    log_grad = log_grad_three.at[-1].add(decay_grad)
    x_conv_grad, entry_grad, read_grad_two, step_grad, grad_skip = pull_two(
        (y_local_grad, state_out_grad, log_grad)
    )
    raw_x_grad, bc_raw_grad, dt_raw_grad, history_grad, grad_conv_x, conv_bc_part, grad_dt_bias = (
        pull_one((x_conv_grad, entry_grad, read_grad_two + read_grad_three, step_grad))
    )
    tail_grad = passed_along(history_grad, "context", -1)
    raw_grad = (
        jnp.concatenate([raw_x_grad, bc_raw_grad], axis=1)
        .at[tok_rows - (CONV - 1) :]
        .add(tail_grad)
    )
    zx_grad = jnp.stack([gate_z_grad, raw_grad[:, :x_width]], axis=1).astype(jnp.bfloat16)
    bc_grad = raw_grad[:, x_width:]
    dt_grad = dt_raw_grad.astype(jnp.bfloat16)
    grad_in_local = jnp.einsum("td,tjc->djc", normed, zx_grad, preferred_element_type=jnp.float32)
    grad_dt_local = jnp.einsum("td,th->dh", normed, dt_grad, preferred_element_type=jnp.float32)
    grad_bc_part = jnp.dot(normed.astype(jnp.float32).T, bc_grad, precision=lax.Precision.HIGHEST)
    normed_grad = normed_grad + jnp.einsum(
        "tjc,djc->td", zx_grad, in_full, preferred_element_type=jnp.float32
    )
    normed_grad = normed_grad + jnp.einsum(
        "th,dh->td", dt_grad, dt_full, preferred_element_type=jnp.float32
    )
    normed_grad = normed_grad + jnp.dot(
        bc_grad, bc_full.astype(jnp.float32).T, precision=lax.Precision.HIGHEST
    )
    normed_sum, grad_bc, conv_bc_sum, down_sum = (
        lax.psum(normed_grad.astype(jnp.bfloat16), "tensor").astype(jnp.float32),
        lax.psum(grad_bc_part.astype(jnp.bfloat16), "tensor").astype(jnp.float32),
        lax.psum(conv_bc_part.astype(jnp.bfloat16), "tensor").astype(jnp.float32),
        lax.psum(down_part.astype(jnp.bfloat16), "tensor").astype(jnp.float32),
    )
    block_out = (resid + down_sum).astype(jnp.bfloat16)
    input_norm_grad, grad_norm_gain = pull_norm_one(normed_sum)
    grad_input = (resid_grad + input_norm_grad).astype(jnp.bfloat16)
    reduced = (
        lax.psum_scatter(grad_in_local, ("shard", "context"), scatter_dimension=0, tiled=True),
        lax.psum_scatter(grad_bc, ("shard", "context"), scatter_dimension=0, tiled=True),
        lax.psum_scatter(grad_dt_local, ("shard", "context"), scatter_dimension=0, tiled=True),
        lax.psum_scatter(grad_mout, ("shard", "context"), scatter_dimension=1, tiled=True),
        lax.psum_scatter(grad_query, ("shard", "context"), scatter_dimension=0, tiled=True),
        lax.psum_scatter(grad_kv, ("shard", "context"), scatter_dimension=0, tiled=True),
        lax.psum_scatter(grad_attn_o, ("shard", "context"), scatter_dimension=1, tiled=True),
        lax.psum_scatter(grad_gate_up, ("shard", "context"), scatter_dimension=0, tiled=True),
        lax.psum_scatter(grad_down, ("shard", "context"), scatter_dimension=1, tiled=True),
    )
    small_norm, small_mlp, small_ssm, small_conv_x, small_conv_bc, small_dt_bias, small_skip = (
        lax.psum(
            (
                grad_norm_gain,
                grad_mlp_gain,
                grad_ssm_gain,
                grad_conv_x,
                conv_bc_sum,
                grad_dt_bias,
                grad_skip,
            ),
            ("shard", "context"),
        )
    )
    return (
        block_out[None],
        grad_input[None],
        small_norm,
        reduced[0],
        reduced[1],
        reduced[2],
        small_dt_bias,
        small_conv_x,
        small_conv_bc,
        small_skip,
        small_ssm,
        reduced[3],
        reduced[4],
        reduced[5],
        reduced[6],
        small_mlp,
        reduced[7],
        reduced[8],
    )


def solution(mesh):
    in_specs = (
        P("shard", "context", None),
        P(),
        P("shard", None, "tensor"),
        P("shard", None),
        P("shard", "tensor"),
        P("tensor"),
        P("tensor"),
        P(None, "tensor"),
        P(),
        P("tensor"),
        P("tensor"),
        P("tensor", "shard"),
        P("shard", "tensor"),
        P("shard", None, "tensor"),
        P("tensor", "shard"),
        P(),
        P("shard", None, "tensor"),
        P("tensor", "shard"),
        P("shard", "context", None),
    )
    out_specs = (
        P("shard", "context", None),
        P("shard", "context", None),
        P(),
        P(("shard", "context"), None, "tensor"),
        P(("shard", "context"), None),
        P(("shard", "context"), "tensor"),
        P("tensor"),
        P(None, "tensor"),
        P(),
        P("tensor"),
        P("tensor"),
        P("tensor", ("shard", "context")),
        P(("shard", "context"), "tensor"),
        P(("shard", "context"), None, "tensor"),
        P("tensor", ("shard", "context")),
        P(),
        P(("shard", "context"), None, "tensor"),
        P("tensor", ("shard", "context")),
    )
    return jax.shard_map(shards, mesh=mesh, in_specs=in_specs, out_specs=out_specs, check_vma=False)
```

profile of v0, /device:TPU:0, one launch (start us, length us, event | category | flops | bytes accessed | tf_op | source)
XLA Modules:
  0.0 1385.4 jit_solution(1702162191112050192)
XLA Ops:
  9.5 9.8 all_gather.56
  23.8 12.3 all_gather.55
  38.3 21.7 %all-gather.10.cloned.1.call-done = bf16[1024,2,768]{2,0,1:T(8,128)(2,1)} async-done(((bf16[256,2,768]{2,0,1:T(8,128)(2,1)}), bf16[1024,2,768]{2,0,1:T(8,128)(2,1)}) %all-gather.10.cloned.1.call-update) | async-done | bytes 3145744 | tf_op jit(solution)/shard_map/all_gather | solution.py:167
  60.0 4.7 copy.135
  83.3 10.0 all_gather.50
  94.7 10.4 all_gather.52
  107.2 12.1 all-gather.2
  119.3 13.9 %all_gather.51 = bf16[1024,128]{0,1:T(8,128)(2,1)S(1)} all-gather(bf16[256,128]{0,1:T(8,128)(2,1)S(1)} %bitcast.488), channel_id=1, replica_groups=mesh['shard'=4,'context'=4,'tensor'=2] {'context'}, dimensions={0}, use_global_device_ids=true | all-gather | bytes 327680 | tf_op jit(solution)/shard_map/all_gather | solution.py:229
  133.1 14.7 %all_gather.53 = bf16[256,1024]{1,0:T(8,128)(2,1)S(1)} all-gather(bf16[256,256]{1,0:T(8,128)(2,1)S(1)} %copy-done.62), channel_id=1, replica_groups=mesh['shard'=4,'context'=4,'tensor'=2] {'shard'}, dimensions={1}, use_global_device_ids=true | all-gather | bytes 655360 | tf_op jit(solution)/shard_map/all_gather | solution.py:173
  161.1 6.3 multiply_reduce_fusion.13
  175.0 31.6 %all-gather.14.cloned.1.call-done = bf16[1024,2,1024]{2,0,1:T(8,128)(2,1)} async-done(((bf16[256,2,1024]{2,0,1:T(8,128)(2,1)}), bf16[1024,2,1024]{2,0,1:T(8,128)(2,1)}) %all-gather.14.cloned.1.call-update) | async-done | bytes 4194320 | tf_op jit(solution)/shard_map/all_gather | solution.py:174
  206.6 6.3 copy.142
  215.8 14.3 %all-reduce.30.cloned.1.call-done = (f32[256,1024]{1,0:T(8,128)}, f32[256,1024]{1,0:T(8,128)}) async-done(((f32[256,1024]{1,0:T(8,128)}, f32[256,1024]{1,0:T(8,128)}), (f32[256,1024]{1,0:T(8,128)}, f32[256,1024]{1,0:T(8,128)})) %all-reduce.30.cloned.1.call-update) | async-done | bytes 2097168 | tf_op jit(solution)/shard_map/psum | solution.py:251
  233.1 4.8 fusion
  237.9 30.4 %all-gather.16.cloned.1.call-done = bf16[1024,1024]{1,0:T(8,128)(2,1)} async-done(((bf16[1024,256]{1,0:T(8,128)(2,1)}), bf16[1024,1024]{1,0:T(8,128)(2,1)}) %all-gather.16.cloned.1.call-update) | async-done | bytes 2097168 | tf_op jit(solution)/shard_map/all_gather | solution.py:175
  275.4 11.1 all-gather.3
  310.0 6.5 fusion.18
  320.1 20.6 %all-gather.1 = bf16[48,64,128]{2,1,0:T(8,128)(2,1)} all-gather(bf16[12,64,128]{2,1,0:T(8,128)(2,1)S(1)} %convolution_convert_fusion.2), channel_id=3, replica_groups=mesh['shard'=4,'context'=4,'tensor'=2] {'context'}, dimensions={0}, use_global_device_ids=true | all-gather | bytes 983040 | tf_op jit(solution)/shard_map/all_gather | solution.py:43
  340.8 5.2 while.29
  408.6 5.7 fusion.93
  417.3 4.4 all-reduce.32.cloned.1.call-done
  426.4 4.5 fusion.99
  434.3 67.6 %reduce-scatter.31.cloned.1.call-done = f32[64,12]{1,0:T(8,128)} async-done(((f32[1024,12]{1,0:T(8,128)}), f32[64,12]{1,0:T(8,128)}) %reduce-scatter.31.cloned.1.call-update) | async-done | bytes 3088
  503.3 76.3 %reduce-scatter.23.cloned.1.call-done = f32[64,2,64]{2,0,1:T(8,128)} async-done(((f32[1024,2,64]{2,0,1:T(8,128)}), f32[64,2,64]{2,0,1:T(8,128)}) %reduce-scatter.23.cloned.1.call-update) | async-done | bytes 32784 | tf_op jit(solution)/shard_map/reduce_scatter | solution.py:383
  582.7 73.5 %all-reduce.21 = (f32[1024]{0:T(1024)}, f32[12]{0:T(128)}, f32[4,768]{1,0:T(4,128)}, f32[4,256]{1,0:T(4,128)}, f32[12]{0:T(128)}, /*index=5*/f32[768]{0:T(1024)}, f32[1024]{0:T(1024)}) all-reduce(f32[1024]{0:T(1024)S(1)} %get-tuple-element.252, ...), channel_id=1, replica_groups=mesh['shard'=4,'context'=4,'tensor'=2] {'shard','context'}, use_global_device_ids=true, to_apply=%region_32.33 | all-reduce | flops 6936 | bytes 53440 | tf_op jit(solution)/shard_map/psum | solution.py:389
  658.9 68.5 %reduce-scatter.15.cloned.1.call-done = f32[64,2,768]{2,0,1:T(8,128)} async-done(((f32[1024,2,768]{2,0,1:T(8,128)}), f32[64,2,768]{2,0,1:T(8,128)}) %reduce-scatter.15.cloned.1.call-update) | async-done | bytes 393232 | tf_op jit(solution)/shard_map/reduce_scatter | solution.py:378
  729.5 181.7 %reduce-scatter.27.cloned.1.call-done = f32[64,2,1024]{2,0,1:T(8,128)} async-done(((f32[1024,2,1024]{2,0,1:T(8,128)}), f32[64,2,1024]{2,0,1:T(8,128)}) %reduce-scatter.27.cloned.1.call-update) | async-done | bytes 524304 | tf_op jit(solution)/shard_map/reduce_scatter | solution.py:385
  913.4 76.9 %reduce-scatter.21.cloned.1.call-done = f32[64,256]{1,0:T(8,128)} async-done(((f32[1024,256]{1,0:T(8,128)}), f32[64,256]{1,0:T(8,128)}) %reduce-scatter.21.cloned.1.call-update) | async-done | bytes 65552 | tf_op jit(solution)/shard_map/reduce_scatter | solution.py:382
  990.3 78.1 %reduce-scatter.25.cloned.1.call-done = f32[256,64]{0,1:T(8,128)} async-done(((f32[256,1024]{0,1:T(8,128)}), f32[256,64]{0,1:T(8,128)}) %reduce-scatter.25.cloned.1.call-update) | async-done | bytes 65552 | tf_op jit(solution)/shard_map/reduce_scatter | solution.py:384
  1068.4 78.1 %reduce-scatter.17.cloned.1.call-done = f32[64,256]{1,0:T(8,128)} async-done(((f32[1024,256]{1,0:T(8,128)}), f32[64,256]{1,0:T(8,128)}) %reduce-scatter.17.cloned.1.call-update) | async-done | bytes 65552 | tf_op jit(solution)/shard_map/reduce_scatter | solution.py:379
  1146.4 133.5 %reduce-scatter.19.cloned.1.call-done = f32[768,64]{0,1:T(8,128)} async-done(((f32[768,1024]{0,1:T(8,128)}), f32[768,64]{0,1:T(8,128)}) %reduce-scatter.19.cloned.1.call-update) | async-done | bytes 196624 | tf_op jit(solution)/shard_map/reduce_scatter | solution.py:381
  1280.0 98.4 %reduce-scatter.29.cloned.1.call-done = f32[1024,64]{0,1:T(8,128)} async-done(((f32[1024,1024]{0,1:T(8,128)}), f32[1024,64]{0,1:T(8,128)}) %reduce-scatter.29.cloned.1.call-update) | async-done | bytes 262160 | tf_op jit(solution)/shard_map/reduce_scatter | solution.py:386
  (462 shorter events, 180.7 us)
Async XLA Ops:
  7.2 52.8 %all-gather.10.cloned.1.call-start = ((), (), s32[]{:S(2)}) async-start(), calls=%async_computation.10 | async-start | bytes 3932160 | tf_op jit(solution)/shard_map/all_gather | solution.py:167
  9.5 150.2 %all-gather.18.cloned.1.call-start = ((), (), s32[]{:S(2)}) async-start(), calls=%async_computation.24 | async-start | bytes 1966080 | tf_op jit(solution)/shard_map/all_gather | solution.py:27
  21.4 129.0 %copy-start.65 = (f32[256]{0:T(256)}, f32[256]{0:T(256)S(1)}, u32[]{:S(2)}) copy-start(f32[256]{0:T(256)S(1)} %fusion.193) | copy-start | bytes 3076
  67.6 232.5 %copy-start.3 = (f32[256,2,768]{2,0,1:T(8,128)}, f32[256,2,768]{2,0,1:T(8,128)S(1)}, u32[]{:S(2)}) copy-start(f32[256,2,768]{2,0,1:T(8,128)S(1)} %fusion.6) | copy-start | bytes 4718596
  68.8 4.8 collective-permute-start
  76.7 84.4 %copy-start.4 = (f32[256,768]{0,1:T(8,128)}, f32[256,768]{0,1:T(8,128)S(1)}, u32[]{:S(2)}) copy-start(f32[256,768]{0,1:T(8,128)S(1)} %copy.136) | copy-start | bytes 2359300
  78.3 81.9 %copy-start.14 = (f32[256,256]{1,0:T(8,128)}, f32[256,256]{1,0:T(8,128)S(1)}, u32[]{:S(2)}) copy-start(f32[256,256]{1,0:T(8,128)S(1)} %get-tuple-element.313) | copy-start | bytes 786436
  79.9 91.1 %all-gather.12.cloned.1.call-start = ((), (), s32[]{:S(2)}) async-start(), calls=%async_computation.11 | async-start | bytes 1966080 | tf_op jit(solution)/shard_map/all_gather | solution.py:170
  80.6 125.9 %all-gather.14.cloned.1.call-start = ((), (), s32[]{:S(2)}) async-start(), calls=%async_computation.12 | async-start | bytes 5242880 | tf_op jit(solution)/shard_map/all_gather | solution.py:174
  83.2 146.9 %all-reduce.30.cloned.1.call-start = ((), (), s32[]{:S(2)}) async-start(), calls=%async_computation.26 | async-start | bytes 4194304 | tf_op jit(solution)/shard_map/psum | solution.py:251
  83.3 68.7 %copy-start.112 = (f32[32]{0:T(128)}, f32[32]{0:T(128)S(1)}, u32[]{:S(2)}) copy-start(f32[32]{0:T(128)S(1)} %multiply_power_fusion) | copy-start | bytes 388
  174.4 94.0 %all-gather.16.cloned.1.call-start = ((), (), s32[]{:S(2)}) async-start(), calls=%async_computation.13 | async-start | bytes 2621440 | tf_op jit(solution)/shard_map/all_gather | solution.py:175
  174.9 120.0 %all-reduce.28.cloned.1.call-start = ((), (), s32[]{:S(2)}) async-start(), calls=%async_computation.14 | async-start | bytes 2097152 | tf_op jit(solution)/shard_map/psum | solution.py:274
  275.2 118.9 %reduce-scatter.13.cloned.1.call-start = ((), (), s32[]{:S(2)}) async-start(), calls=%async_computation.15 | async-start | bytes 327680 | tf_op jit(solution)/shard_map/reduce_scatter | solution.py:303
  369.2 14.9 %collective-permute-start.1 = (f32[3,1024]{1,0:T(4,128)}, f32[3,1024]{1,0:T(4,128)}, u32[]{:S(2)}, u32[]{:S(2)}) collective-permute-start(f32[3,1024]{1,0:T(4,128)} %pad_add_fusion.2), channel_id=1, source_target_pairs={{2,0},{4,2},{6,4},{3,1},{5,3},{7,5},{10,8},{12,10},{14,12},{11,9},... | collective-permute-start | bytes 36872 | tf_op jit(solution)/shard_map/ppermute | solution.py:22
  371.3 50.4 %all-reduce.32.cloned.1.call-start = ((), (), s32[]{:S(2)}) async-start(), calls=%async_computation.27 | async-start | bytes 3145728 | tf_op jit(solution)/shard_map/psum | solution.py:372
  400.8 101.1 %reduce-scatter.31.cloned.1.call-start = ((), (), s32[]{:S(2)}) async-start(), calls=%async_computation.25 | async-start | bytes 557056
  402.1 177.5 %reduce-scatter.23.cloned.1.call-start = ((), (), s32[]{:S(2)}) async-start(), calls=%async_computation.20 | async-start | bytes 1114112 | tf_op jit(solution)/shard_map/reduce_scatter | solution.py:383
  403.7 323.8 %reduce-scatter.15.cloned.1.call-start = ((), (), s32[]{:S(2)}) async-start(), calls=%async_computation.16 | async-start | bytes 6684672 | tf_op jit(solution)/shard_map/reduce_scatter | solution.py:378
  407.6 503.6 %reduce-scatter.27.cloned.1.call-start = ((), (), s32[]{:S(2)}) async-start(), calls=%async_computation.22 | async-start | bytes 8912896 | tf_op jit(solution)/shard_map/reduce_scatter | solution.py:385
  414.3 576.0 %reduce-scatter.21.cloned.1.call-start = ((), (), s32[]{:S(2)}) async-start(), calls=%async_computation.19 | async-start | bytes 1114112 | tf_op jit(solution)/shard_map/reduce_scatter | solution.py:382
  415.9 652.5 %reduce-scatter.25.cloned.1.call-start = ((), (), s32[]{:S(2)}) async-start(), calls=%async_computation.21 | async-start | bytes 1114112 | tf_op jit(solution)/shard_map/reduce_scatter | solution.py:384
  417.3 729.2 %reduce-scatter.17.cloned.1.call-start = ((), (), s32[]{:S(2)}) async-start(), calls=%async_computation.17 | async-start | bytes 1114112 | tf_op jit(solution)/shard_map/reduce_scatter | solution.py:379
  423.8 856.2 %reduce-scatter.19.cloned.1.call-start = ((), (), s32[]{:S(2)}) async-start(), calls=%async_computation.18 | async-start | bytes 3342336 | tf_op jit(solution)/shard_map/reduce_scatter | solution.py:381
  426.3 952.1 %reduce-scatter.29.cloned.1.call-start = ((), (), s32[]{:S(2)}) async-start(), calls=%async_computation.23 | async-start | bytes 4456448 | tf_op jit(solution)/shard_map/reduce_scatter | solution.py:386
  430.9 151.7 %copy-start.87 = (f32[1024]{0:T(1024)S(1)}, f32[1024]{0:T(1024)}, u32[]{:S(2)}) copy-start(f32[1024]{0:T(1024)} %get-tuple-element.247) | copy-start | bytes 12292
  430.9 151.7 %copy-start.117 = (f32[768]{0:T(1024)S(1)}, f32[768]{0:T(1024)}, u32[]{:S(2)}) copy-start(f32[768]{0:T(1024)} %get-tuple-element.318) | copy-start | bytes 9220
  430.9 151.7 %copy-start.124 = (f32[12]{0:T(128)S(1)}, f32[12]{0:T(128)}, u32[]{:S(2)}) copy-start(f32[12]{0:T(128)} %get-tuple-element.303) | copy-start | bytes 148
  431.0 225.2 %copy-start.105 = (f32[256]{0:T(256)S(1)}, f32[256]{0:T(256)}, u32[]{:S(2)}) copy-start(f32[256]{0:T(256)} %copy-done.104) | copy-start | bytes 3076
  431.0 225.2 %copy-start.8 = (f32[256,1024]{1,0:T(8,128)S(1)}, f32[256,1024]{1,0:T(8,128)}, u32[]{:S(2)}) copy-start(f32[256,1024]{1,0:T(8,128)} %all-reduce.28.cloned.1.call-done) | copy-start | bytes 3145732
  431.0 225.2 %copy-start.27 = (bf16[1,256,1024]{2,1,0:T(8,128)(2,1)S(1)}, bf16[1,256,1024]{2,1,0:T(8,128)(2,1)}, u32[]{:S(2)}) copy-start(bf16[1,256,1024]{2,1,0:T(8,128)(2,1)} %param.45) | copy-start | bytes 1572868
  431.0 225.2 %copy-start.97 = (f32[256]{0:T(256)S(1)}, f32[256]{0:T(256)}, u32[]{:S(2)}) copy-start(f32[256]{0:T(256)} %copy-done.96) | copy-start | bytes 3076
  (114 other events, 984.6 us)
Sparse Core Ops, SparseCore 0:
  9.9 50.0 all-gather.9
  80.0 38.2 all-gather.17
  120.1 33.4 all-gather.11
  155.3 51.2 all-gather.13
  208.8 21.2 all-reduce.29
  232.0 36.3 all-gather.15
  275.3 19.5 all-reduce.27
  371.4 19.9 reduce-scatter.12
  400.9 20.7 all-reduce.31
  423.8 78.0 reduce-scatter.30
  504.3 75.2 reduce-scatter.22
  584.7 142.6 reduce-scatter.14
  729.7 181.4 reduce-scatter.26
  913.9 76.3 reduce-scatter.20
  993.1 75.2 reduce-scatter.24
  1071.1 75.3 reduce-scatter.16
  1152.6 127.3 reduce-scatter.18
  1282.8 95.5 reduce-scatter.28
where the time goes:
time: 1400 us; the launch traced here: 1390 us
  waiting for transfers between devices  968 us (69%)
  blocking collectives  193 us (14%)
  matrix products  101 us (7%)
  local copies, waits for them, and re-layouts  51 us (4%)
  other arithmetic  50.6 us (4%)
  between operations  16.4 us (1%)
    reduce_scatter x1, waiting for transfers between devices, shards(): lax.psum_scatter(grad_gate_up, ('shard', 'context'), scatter_dimension=0,...  182 us
    reduce_scatter x1, waiting for transfers between devices, shards(): lax.psum_scatter(grad_mout, ('shard', 'context'), scatter_dimension=1, ti...  134 us
    reduce_scatter x1, waiting for transfers between devices, shards(): lax.psum_scatter(grad_down, ('shard', 'context'), scatter_dimension=1, ti...  98.4 us
    reduce_scatter x1, waiting for transfers between devices, shards(): lax.psum_scatter(grad_bc, ('shard', 'context'), scatter_dimension=0, tile...  78.1 us
    reduce_scatter x1, waiting for transfers between devices, shards(): lax.psum_scatter(grad_attn_o, ('shard', 'context'), scatter_dimension=1,...  78.1 us
    reduce_scatter x1, waiting for transfers between devices, shards(): lax.psum_scatter(grad_query, ('shard', 'context'), scatter_dimension=0, t...  76.9 us
    reduce_scatter x1, waiting for transfers between devices, shards(): lax.psum_scatter(grad_kv, ('shard', 'context'), scatter_dimension=0, tile...  76.3 us
    psum x1, blocking collectives, shards(): lax.psum((grad_norm_gain, grad_mlp_gain, grad_ssm_gain, grad_conv_x, conv...  73.5 us
  transfers between devices with their start and end apart: 20, of which 16 were waited for; matrix products, arithmetic and copies ran while one was open for 8% of the time, Pallas kernels for 0%

commit v1 on v0

v1 whole, which is shorter than its diff:
```python
from functools import partial

import jax
import jax.numpy as jnp
from jax import lax
from jax.sharding import PartitionSpec as P

D = 1024
HD = 64
STATE = 128
CONV = 4
DSSM = 1536


epsilon = 1e-05
rope_base = 100000000000.0


def passed_along(block, axis, distance):
    devices = range(lax.axis_size(axis))
    route = [(i - distance, i) for i in devices if i - distance in devices]
    return lax.ppermute(block, axis, route)


def swapped(block, axis, bit):
    return lax.ppermute(block, axis, [(i, i ^ bit) for i in range(lax.axis_size(axis))])


def bits_of(axis):
    return [1 << k for k in range(lax.axis_size(axis).bit_length() - 1)]


def pair_sum(block):
    return block + swapped(block, "tensor", 1).astype(block.dtype)


def near_first(values):
    count = lax.axis_size("shard")
    own = lax.axis_index("shard")
    width = values.shape[-1] // count
    return jnp.concatenate(
        [
            lax.dynamic_slice_in_dim(values, (own ^ j) * width, width, axis=values.ndim - 1)
            for j in range(count)
        ],
        axis=-1,
    )


def gathered_rows(block):
    bits = bits_of("shard")
    half = block.shape[0] // 2
    halves = []
    for part, order in ((block[:half], bits), (block[half:], bits[::-1])):
        pieces = {0: part}
        for bit in order:
            pieces.update({j ^ bit: swapped(p, "shard", bit) for j, p in list(pieces.items())})
        halves.append(pieces)
    return jnp.concatenate(
        [pieces[j] for j in range(lax.axis_size("shard")) for pieces in halves], axis=0
    )


def reduced_rows(left, right):
    count = lax.axis_size("shard")
    width = left.shape[1] // count
    columns = right.shape[1]
    cut = columns // 256 * 128
    bits = bits_of("shard")
    outs = []
    for part, order in ((right[:, :cut], bits), (right[:, cut:], bits[::-1])):
        pieces = {
            j: jnp.einsum(
                "td,tc->dc",
                left[:, j * width : (j + 1) * width],
                part,
                preferred_element_type=jnp.float32,
            )
            for j in range(count)
        }
        for bit in order:
            sent = {j: pieces.pop(j) for j in list(pieces) if j & bit}
            for j, piece in sent.items():
                pieces[j ^ bit] = pieces[j ^ bit] + swapped(
                    piece.astype(jnp.bfloat16), "shard", bit
                ).astype(jnp.float32)
        total = pieces[0]
        place = lax.axis_index("context")
        for bit in bits_of("context")[::-1]:
            rows = total.shape[0] // 2
            upper = (place // bit) % 2
            sent = lax.dynamic_slice_in_dim(total, (1 - upper) * rows, rows, axis=0)
            kept = lax.dynamic_slice_in_dim(total, upper * rows, rows, axis=0)
            total = kept + swapped(sent.astype(jnp.bfloat16), "context", bit).astype(jnp.float32)
        outs.append(total)
    return jnp.concatenate(outs, axis=1)


def summed_everywhere(block):
    for axis in ("shard", "context"):
        for bit in bits_of(axis):
            block = block + swapped(block, axis, bit)
    return block


def packed_state(decay, state):
    high = decay.astype(jnp.bfloat16)
    low = (decay - high.astype(jnp.float32)).astype(jnp.bfloat16)
    head = jnp.pad(jnp.stack([high, low]), ((0, 14), (0, STATE - decay.shape[0])))
    return jnp.concatenate([head, state.reshape(-1, STATE).astype(jnp.bfloat16)], axis=0)


def unpacked_state(packed, heads):
    decay = packed[0, :heads].astype(jnp.float32) + packed[1, :heads].astype(jnp.float32)
    return (decay, packed[16:].reshape(heads, HD, STATE).astype(jnp.float32))


def carried_state(decay, state, direction):
    heads = decay.shape[0]
    packed = packed_state(decay, state)
    weight = jnp.ones_like(decay)
    total = jnp.zeros_like(state)
    for distance in range(1, lax.axis_size("context")):
        far_decay, far_state = unpacked_state(
            passed_along(packed, "context", direction * distance), heads
        )
        total = total + weight[:, None, None] * far_state
        weight = weight * far_decay
    return total


def rms_scale(values, gain):
    return values * lax.rsqrt(jnp.mean(values * values, axis=-1, keepdims=True) + epsilon) * gain


def rotate(values, positions):
    half_dim = values.shape[-1] // 2
    frequency = rope_base ** (-2.0 * jnp.arange(half_dim, dtype=jnp.float32) / values.shape[-1])
    angles = positions[:, None] * frequency[None, :]
    cosine = jnp.cos(angles)[:, None, :]
    sine_part = jnp.sin(angles)[:, None, :]
    lower_half = values[..., :half_dim]
    upper_half = values[..., half_dim:]
    return jnp.concatenate(
        [
            lower_half * cosine - upper_half * sine_part,
            upper_half * cosine + lower_half * sine_part,
        ],
        axis=-1,
    )


def conv_silu(raw, history, weight):
    padded = jnp.concatenate([history, raw], axis=0)
    row_count = raw.shape[0]
    conv_sum = sum(
        (
            weight[kernel_step] * padded[kernel_step : kernel_step + row_count]
            for kernel_step in range(weight.shape[0])
        )
    )
    return jax.nn.silu(conv_sum)


def swiglu(gate_part, up_part):
    return jax.nn.silu(gate_part) * up_part


def section_one(raw_x, raw_bc, dt_raw, history, conv_x, conv_bc, dt_bias):
    x_width = raw_x.shape[1]
    x_conv = conv_silu(raw_x, history[:, :x_width], conv_x)
    bc_conv = conv_silu(raw_bc, history[:, x_width:], conv_bc)
    step_size = jax.nn.softplus(dt_raw + dt_bias)
    return (x_conv, bc_conv[:, :STATE], bc_conv[:, STATE:], step_size)


def section_two(x_conv, entry_map, read_map, step_size, skip_d, decay_rate):
    row_count = step_size.shape[0]
    head_count = step_size.shape[1]
    x_heads = x_conv.reshape(row_count, head_count, HD)
    log_decay = jnp.cumsum(step_size * decay_rate, axis=0)
    causal = jnp.arange(row_count)[:, None] >= jnp.arange(row_count)[None, :]
    gap_log = log_decay.T[:, :, None] - log_decay.T[:, None, :]
    decay_mask = jnp.where(causal, jnp.exp(jnp.where(causal, gap_log, 0.0)), 0.0)
    scores = jnp.dot(read_map, entry_map.T, precision=lax.Precision.HIGH)
    weighted = x_heads * step_size[:, :, None]
    inner_part = jnp.einsum(
        "hts,shp->thp", decay_mask * scores, weighted, precision=lax.Precision.HIGH
    )
    tail_weight = jnp.exp(log_decay[-1][None, :] - log_decay) * step_size
    local_state = jnp.einsum(
        "sh,shp,sn->hpn", tail_weight, x_heads, entry_map, precision=lax.Precision.HIGH
    )
    return (inner_part + skip_d[None, :, None] * x_heads, local_state, log_decay)


def section_three(y_local, state_in, read_map, log_decay, gate_z):
    carried = (
        jnp.einsum("tn,hpn->thp", read_map, state_in, precision=lax.Precision.HIGH)
        * jnp.exp(log_decay)[:, :, None]
    )
    ssm_out = (y_local + carried).reshape(y_local.shape[0], -1)
    return ssm_out * jax.nn.silu(gate_z)


def shards(
    hidden_in,
    norm_gain,
    mamba_in,
    mamba_bc,
    mamba_dt,
    dt_bias,
    decay_seed,
    conv_x,
    conv_bc,
    skip_d,
    ssm_gain,
    mamba_out,
    attn_q,
    attn_kv,
    attn_out,
    mlp_gain,
    mlp_gate_up,
    mlp_down,
    cotangent,
):
    rows_own = mamba_in.shape[0]
    x_width = mamba_in.shape[2]
    heads = mamba_dt.shape[1]
    dt_width = -(-heads // 128) * 128
    q_width = attn_q.shape[1]
    kv_width = attn_kv.shape[2]
    ff_local = mlp_gate_up.shape[2]
    scan_full = gathered_rows(
        jnp.concatenate(
            [mamba_in[:, 1], mamba_bc, jnp.pad(mamba_dt, ((0, 0), (0, dt_width - heads)))], axis=1
        )
    )
    side_full = gathered_rows(
        jnp.concatenate([mamba_in[:, 0], attn_q, attn_kv.reshape(rows_own, 2 * kv_width)], axis=1)
    )
    mix_full = gathered_rows(jnp.concatenate([mamba_out.T, attn_out.T], axis=1))
    mlp_full = gathered_rows(
        jnp.concatenate([mlp_gate_up.reshape(rows_own, 2 * ff_local), mlp_down.T], axis=1)
    )
    gu_full = mlp_full[:, : 2 * ff_local]
    down_full = mlp_full[:, 2 * ff_local :]
    mout_full = mix_full[:, :x_width]
    attn_full = mix_full[:, x_width:]
    norm_gain = near_first(norm_gain)
    mlp_gain = near_first(mlp_gain)
    row_in = near_first(hidden_in[0]).astype(jnp.float32)
    out_grad = near_first(cotangent[0])
    tok_rows = row_in.shape[0]
    seq_len = tok_rows * lax.axis_size("context")
    positions_int = lax.axis_index("context") * tok_rows + jnp.arange(tok_rows, dtype=jnp.int32)
    positions = positions_int.astype(jnp.float32)
    score_scale = HD ** (-0.5)
    normed_f, pull_norm_one = jax.vjp(rms_scale, row_in, norm_gain)
    normed = normed_f.astype(jnp.bfloat16)
    scan_proj = jnp.dot(normed, scan_full, preferred_element_type=jnp.float32)
    raw_x = scan_proj[:, :x_width]
    bc_raw = scan_proj[:, x_width : x_width + 2 * STATE]
    dt_raw = scan_proj[:, x_width + 2 * STATE : x_width + 2 * STATE + heads]
    side_proj = jnp.dot(normed, side_full, preferred_element_type=jnp.float32)
    gate_z = side_proj[:, :x_width]
    history = passed_along(
        scan_proj[tok_rows - (CONV - 1) :, : x_width + 2 * STATE], "context", 1
    )
    decay_rate = -jnp.exp(0.5 * decay_seed.astype(jnp.float32)) / seq_len
    (x_conv, entry_map, read_map, step_size), pull_one = jax.vjp(
        section_one, raw_x, bc_raw, dt_raw, history, conv_x, conv_bc, dt_bias
    )
    (y_local, state_local, log_decay), pull_two = jax.vjp(
        partial(section_two, decay_rate=decay_rate), x_conv, entry_map, read_map, step_size, skip_d
    )
    block_decay = jnp.exp(log_decay[-1])
    state_in = carried_state(block_decay, state_local, 1)
    gated_y, pull_three = jax.vjp(
        section_three, y_local, state_in, read_map, log_decay, gate_z
    )
    gated_b = (gated_y * ssm_gain).astype(jnp.bfloat16)
    mamba_part = jnp.einsum("tc,dc->td", gated_b, mout_full, preferred_element_type=jnp.float32)
    square_part = jnp.sum(gated_y * gated_y, axis=-1)
    query_heads = q_width // HD
    kv_heads = kv_width // HD
    group_size = query_heads // kv_heads
    query_pre = side_proj[:, x_width : x_width + q_width].reshape(
        tok_rows, query_heads, HD
    )
    queries = (
        rotate(query_pre, positions)
        .astype(jnp.bfloat16)
        .reshape(tok_rows, kv_heads, group_size, HD)
    )
    kv_pre = side_proj[:, x_width + q_width :].reshape(tok_rows, 2, kv_heads, HD)
    keys_local = rotate(kv_pre[:, 0], positions).astype(jnp.bfloat16)
    values_local = kv_pre[:, 1].astype(jnp.bfloat16)
    kv_send = jnp.stack([keys_local, values_local], axis=1).reshape(tok_rows, 2 * kv_heads * HD)
    blocks = lax.axis_size("context")
    kv_every = jnp.concatenate(
        [kv_send] + [passed_along(kv_send, "context", k) for k in range(1, blocks)], axis=0
    ).reshape(seq_len, 2, kv_heads, HD)
    keys_all = kv_every[:, 0]
    values_all = kv_every[:, 1]
    key_index = jnp.arange(seq_len, dtype=jnp.int32)
    back = key_index // tok_rows
    key_positions = (lax.axis_index("context") - back) * tok_rows + key_index % tok_rows
    allowed = (key_positions >= 0)[None, :] & (key_positions[None, :] <= positions_int[:, None])
    raw_scores = (
        jnp.einsum("tkgd,skd->kgts", queries, keys_all, preferred_element_type=jnp.float32)
        * score_scale
    )
    scores = jnp.where(allowed[None, None], raw_scores, -1e30)
    log_total = jax.nn.logsumexp(scores, axis=-1, keepdims=True)
    probs = jnp.exp(scores - log_total)
    probs_b = probs.astype(jnp.bfloat16)
    attn_vals = jnp.einsum(
        "kgts,skd->tkgd", probs_b, values_all, preferred_element_type=jnp.float32
    )
    attn_vals = attn_vals.astype(jnp.bfloat16).reshape(tok_rows, query_heads * HD)
    attn_part = jnp.einsum("th,dh->td", attn_vals, attn_full, preferred_element_type=jnp.float32)
    attn_sum = pair_sum(attn_part)
    mamba_sum = pair_sum(mamba_part)
    square_sum = pair_sum(square_part)
    ssm_scale = lax.rsqrt(square_sum / DSSM + epsilon)[:, None]
    resid = row_in + (attn_sum + ssm_scale * mamba_sum)
    normed_two_f, pull_norm_two = jax.vjp(rms_scale, resid, mlp_gain)
    normed_two = normed_two_f.astype(jnp.bfloat16)
    gate_up = jnp.dot(normed_two, gu_full, preferred_element_type=jnp.float32)
    hidden_f, pull_gate = jax.vjp(swiglu, gate_up[:, :ff_local], gate_up[:, ff_local:])
    hidden = hidden_f.astype(jnp.bfloat16)
    down_part = jnp.einsum("tf,df->td", hidden, down_full, preferred_element_type=jnp.float32)
    hidden_grad = jnp.dot(out_grad, down_full, preferred_element_type=jnp.float32)
    gate_grad, up_grad = pull_gate(hidden_grad)
    gate_up_grad = jnp.concatenate([gate_grad, up_grad], axis=1).astype(jnp.bfloat16)
    grad_down = reduced_rows(out_grad, hidden)
    grad_gate_up = reduced_rows(normed_two, gate_up_grad)
    normed_two_part = jnp.einsum(
        "tf,df->td", gate_up_grad, gu_full, preferred_element_type=jnp.float32
    )
    normed_two_grad = pair_sum(normed_two_part)
    resid_norm_grad, grad_mlp_gain = pull_norm_two(normed_two_grad)
    resid_grad = out_grad.astype(jnp.float32) + resid_norm_grad
    mixed_grad = resid_grad.astype(jnp.bfloat16)
    grad_attn_o = reduced_rows(mixed_grad, attn_vals)
    vals_grad = jnp.dot(mixed_grad, attn_full, preferred_element_type=jnp.float32)
    vals_grad = vals_grad.astype(jnp.bfloat16).reshape(tok_rows, kv_heads, group_size, HD)
    probs_grad = jnp.einsum(
        "tkgd,skd->kgts", vals_grad, values_all, preferred_element_type=jnp.float32
    )
    score_grad = (
        probs * (probs_grad - jnp.sum(probs * probs_grad, axis=-1, keepdims=True))
    ).astype(jnp.bfloat16)
    query_grad = (
        jnp.einsum("kgts,skd->tkgd", score_grad, keys_all, preferred_element_type=jnp.float32)
        * score_scale
    )
    key_grad_all = (
        jnp.einsum("kgts,tkgd->skd", score_grad, queries, preferred_element_type=jnp.float32)
        * score_scale
    )
    value_grad_all = jnp.einsum(
        "kgts,tkgd->skd", probs_b, vals_grad, preferred_element_type=jnp.float32
    )
    kv_grad_send = jnp.stack([key_grad_all, value_grad_all], axis=1).reshape(
        blocks, tok_rows, 2 * kv_heads * HD
    )
    kv_grad = kv_grad_send[0]
    for k in range(1, blocks):
        kv_grad = kv_grad + passed_along(
            kv_grad_send[k].astype(jnp.bfloat16), "context", -k
        ).astype(jnp.float32)
    kv_grad = kv_grad.reshape(tok_rows, 2, kv_heads, HD)
    query_pre_grad = rotate(query_grad.reshape(tok_rows, query_heads, HD), -positions)
    query_pre_grad = query_pre_grad.reshape(tok_rows, query_heads * HD).astype(jnp.bfloat16)
    key_pre_grad = rotate(kv_grad[:, 0], -positions)
    kv_pre_grad = (
        jnp.stack([key_pre_grad, kv_grad[:, 1]], axis=1)
        .reshape(tok_rows, 2 * kv_heads * HD)
        .astype(jnp.bfloat16)
    )
    mixed_f = mixed_grad.astype(jnp.float32)
    scale_grad = jnp.sum(mixed_f * mamba_sum, axis=-1, keepdims=True)
    mamba_grad = (ssm_scale * mixed_f).astype(jnp.bfloat16)
    grad_mout = reduced_rows(mamba_grad, gated_b)
    gated_grad = jnp.dot(mamba_grad, mout_full, preferred_element_type=jnp.float32)
    grad_ssm_gain = jnp.sum(gated_grad * gated_y, axis=0)
    y_grad = gated_grad * ssm_gain - scale_grad * ssm_scale * ssm_scale * ssm_scale * gated_y / DSSM
    y_local_grad, state_in_grad, read_grad_three, log_grad_three, gate_z_grad = pull_three(y_grad)
    state_out_grad = carried_state(block_decay, state_in_grad, -1)
    decay_grad = block_decay * jnp.sum(state_out_grad * state_in, axis=(1, 2))
    log_grad = log_grad_three.at[-1].add(decay_grad)
    x_conv_grad, entry_grad, read_grad_two, step_grad, grad_skip = pull_two(
        (y_local_grad, state_out_grad, log_grad)
    )
    raw_x_grad, bc_raw_grad, dt_raw_grad, history_grad, grad_conv_x, conv_bc_part, grad_dt_bias = (
        pull_one((x_conv_grad, entry_grad, read_grad_two + read_grad_three, step_grad))
    )
    tail_grad = passed_along(history_grad, "context", -1)
    raw_grad = (
        jnp.concatenate([raw_x_grad, bc_raw_grad], axis=1)
        .at[tok_rows - (CONV - 1) :]
        .add(tail_grad)
    )
    side_grad = jnp.concatenate(
        [gate_z_grad.astype(jnp.bfloat16), query_pre_grad, kv_pre_grad], axis=1
    )
    scan_grad = jnp.concatenate(
        [raw_grad, jnp.pad(dt_raw_grad, ((0, 0), (0, dt_width - heads)))], axis=1
    ).astype(jnp.bfloat16)
    side_total = reduced_rows(normed, side_grad)
    scan_total = reduced_rows(normed, scan_grad)
    normed_grad = jnp.einsum("tc,dc->td", side_grad, side_full, preferred_element_type=jnp.float32)
    normed_grad = normed_grad + jnp.einsum(
        "tc,dc->td", scan_grad, scan_full, preferred_element_type=jnp.float32
    )
    normed_sum = pair_sum(normed_grad)
    grad_bc = pair_sum(scan_total[:, x_width : x_width + 2 * STATE])
    down_sum = pair_sum(down_part)
    block_out = (resid + down_sum).astype(jnp.bfloat16)
    input_norm_grad, grad_norm_gain = pull_norm_one(normed_sum)
    grad_input = (resid_grad + input_norm_grad).astype(jnp.bfloat16)
    small = (
        near_first(grad_norm_gain),
        near_first(grad_mlp_gain),
        grad_ssm_gain,
        grad_conv_x,
        pair_sum(conv_bc_part),
        grad_dt_bias,
        grad_skip,
    )
    flat = jnp.concatenate([item.reshape(-1) for item in small])
    flat = jnp.pad(flat, (0, -flat.shape[0] % 1024)).reshape(-1, 128)
    flat = summed_everywhere(flat).reshape(-1)
    totals = []
    start = 0
    for item in small:
        totals.append(flat[start : start + item.size].reshape(item.shape))
        start += item.size
    small_norm, small_mlp, small_ssm, small_conv_x, small_conv_bc, small_dt_bias, small_skip = (
        totals
    )
    grad_in = jnp.stack([side_total[:, :x_width], scan_total[:, :x_width]], axis=1)
    return (
        near_first(block_out)[None],
        near_first(grad_input)[None],
        small_norm,
        grad_in,
        grad_bc,
        scan_total[:, x_width + 2 * STATE : x_width + 2 * STATE + heads],
        small_dt_bias,
        small_conv_x,
        small_conv_bc,
        small_skip,
        small_ssm,
        grad_mout.T,
        side_total[:, x_width : x_width + q_width],
        side_total[:, x_width + q_width :].reshape(-1, 2, kv_width),
        grad_attn_o.T,
        small_mlp,
        grad_gate_up.reshape(-1, 2, ff_local),
        grad_down.T,
    )


def solution(mesh):
    in_specs = (
        P("shard", "context", None),
        P(),
        P("shard", None, "tensor"),
        P("shard", None),
        P("shard", "tensor"),
        P("tensor"),
        P("tensor"),
        P(None, "tensor"),
        P(),
        P("tensor"),
        P("tensor"),
        P("tensor", "shard"),
        P("shard", "tensor"),
        P("shard", None, "tensor"),
        P("tensor", "shard"),
        P(),
        P("shard", None, "tensor"),
        P("tensor", "shard"),
        P("shard", "context", None),
    )
    out_specs = (
        P("shard", "context", None),
        P("shard", "context", None),
        P(),
        P(("shard", "context"), None, "tensor"),
        P(("shard", "context"), None),
        P(("shard", "context"), "tensor"),
        P("tensor"),
        P(None, "tensor"),
        P(),
        P("tensor"),
        P("tensor"),
        P("tensor", ("shard", "context")),
        P(("shard", "context"), "tensor"),
        P(("shard", "context"), None, "tensor"),
        P("tensor", ("shard", "context")),
        P(),
        P(("shard", "context"), None, "tensor"),
        P("tensor", ("shard", "context")),
    )
    return jax.shard_map(shards, mesh=mesh, in_specs=in_specs, out_specs=out_specs, check_vma=False)
```

time: 1400 us -> 570 us (0.41)
  waiting for transfers between devices: 968 us -> 206 us
  blocking collectives: 193 us -> 0 us
  starting transfers between devices: 5.41 us -> 113 us
  local copies, waits for them, and re-layouts: 51 us -> 78.2 us
  other arithmetic: 50.6 us -> 68.2 us
    reduce_scatter x9 -> x0, waiting for transfers between devices: 791 us -> none  [the longest x1 182 us: shards(): lax.psum_scatter(grad_gate_up, ('shard', 'context'), scatter_dimension=0,...]
    ppermute x0 -> x96, waiting for transfers between devices: none -> 198 us  [swapped(): lax.ppermute(block, axis, [(i, i ^ bit) for i in range(lax.axis_size(axis...]
    all_gather x9 -> x0, blocking collectives: 115 us -> none  [the longest x2 31.7 us: prefix(): lax.all_gather(a.astype(kind), axis)]
    ppermute x0 -> x96, starting transfers between devices: none -> 87.4 us  [swapped(): lax.ppermute(block, axis, [(i, i ^ bit) for i in range(lax.axis_size(axis...]
    all_gather x5 -> x0, waiting for transfers between devices: 83.7 us -> none  [the longest x1 31.6 us: shards(): lax.all_gather(mlp_gate_up, 'shard', axis=0, tiled=True)]
    psum x3 -> x0, blocking collectives: 78.4 us -> none  [the longest x1 73.5 us: shards(): lax.psum((grad_norm_gain, grad_mlp_gain, grad_ssm_gain, grad_conv_x, conv...]
    unnamed x19 -> x0, waiting for transfers between devices: 69 us -> none
    psum x3 -> x0, waiting for transfers between devices: 22 us -> none  [the longest x1 14.3 us: shards(): lax.psum((attn_part, mamba_part, square_part), 'tensor')]
  transfers between devices with their start and end apart: 20 -> 110, of which waited for: 16 -> 55; matrix products, arithmetic and copies ran while one was open for 8% -> 36% of each run, Pallas kernels for 0% -> 0%
where the time goes in v1:
time: 570 us; the launch traced here: 560 us
  waiting for transfers between devices  206 us (36%)
  starting transfers between devices  113 us (20%)
  matrix products  89.4 us (16%)
  local copies, waits for them, and re-layouts  78.2 us (14%)
  other arithmetic  68.2 us (12%)
    ppermute x96, waiting for transfers between devices, swapped(): lax.ppermute(block, axis, [(i, i ^ bit) for i in range(lax.axis_size(axis...  198 us
    ppermute x96, starting transfers between devices, swapped(): lax.ppermute(block, axis, [(i, i ^ bit) for i in range(lax.axis_size(axis...  87.4 us
    dot_general x48, matrix products, reduced_rows(): jnp.einsum('td,tc->dc', left[:, j * width:(j + 1) * width], part, preferr...  41.1 us
    unnamed x439, local copies, waits for them, and re-layouts  35.8 us
    ppermute x14, starting transfers between devices, passed_along(): return lax.ppermute(block, axis, route)  26 us
    dot_general x3, matrix products, section_two(): jnp.einsum('hts,shp->thp', decay_mask * scores, weighted, precision=lax.P...  11.8 us
  transfers between devices with their start and end apart: 110, of which 55 were waited for; matrix products, arithmetic and copies ran while one was open for 36% of the time, Pallas kernels for 0%

profile of v1, /device:TPU:0, one launch (start us, length us, event | category | flops | bytes accessed | tf_op | source)
XLA Modules:
  0.0 559.6 jit_solution(13055931554948273310)
XLA Ops:
  50.5 4.2 collective-permute-done.1
  59.3 20.3 %collective-permute-done.13 = bf16[128,1024]{0,1:T(8,128)(2,1)S(1)} collective-permute-done((bf16[128,1024]{0,1:T(8,128)(2,1)}, bf16[128,1024]{0,1:T(8,128)(2,1)S(1)}, u32[]{:S(2)}, u32[]{:S(2)}) %collective-permute-start.13) | collective-permute-done | bytes 262176 | tf_op jit(solution)/shard_map/ppermute | solution.py:26
  99.9 6.1 %collective-permute-start.8 = (bf16[256,128]{0,1:T(8,128)(2,1)}, bf16[256,128]{0,1:T(8,128)(2,1)}, u32[]{:S(2)}, u32[]{:S(2)}) collective-permute-start(bf16[256,128]{0,1:T(8,128)(2,1)} %bitcast.12), channel_id=1, source_target_pairs={{0,6},{1,7},{8,14},{9,15},{16,22},{17,23},{24,30},{25,31}} | collective-permute-start | bytes 196616 | tf_op jit(solution)/shard_map/ppermute | solution.py:22
  186.5 5.1 collective-permute-done.106
  205.5 8.5 %collective-permute-done.102 = bf16[256,512]{1,0:T(8,128)(2,1)S(1)} collective-permute-done((bf16[256,512]{1,0:T(8,128)(2,1)S(1)}, bf16[256,512]{1,0:T(8,128)(2,1)S(1)}, u32[]{:S(2)}, u32[]{:S(2)}) %collective-permute-start.102) | collective-permute-done | bytes 262176 | tf_op jit(solution)/shard_map/ppermute | solution.py:26
  217.4 11.4 %collective-permute-done.91 = bf16[256,1024]{1,0:T(8,128)(2,1)S(1)} collective-permute-done((bf16[256,1024]{1,0:T(8,128)(2,1)S(1)}, bf16[256,1024]{1,0:T(8,128)(2,1)S(1)}, u32[]{:S(2)}, u32[]{:S(2)}) %collective-permute-start.91) | collective-permute-done | bytes 524320 | tf_op jit(solution)/shard_map/ppermute | solution.py:26
  229.9 7.5 %collective-permute-done.108 = bf16[128,512]{1,0:T(8,128)(2,1)S(1)} collective-permute-done((bf16[128,512]{1,0:T(8,128)(2,1)S(1)}, bf16[128,512]{1,0:T(8,128)(2,1)S(1)}, u32[]{:S(2)}, u32[]{:S(2)}) %collective-permute-start.108) | collective-permute-done | bytes 131104 | tf_op jit(solution)/shard_map/ppermute | solution.py:26
  237.5 5.8 %collective-permute-done.103 = bf16[128,512]{1,0:T(8,128)(2,1)S(1)} collective-permute-done((bf16[128,512]{1,0:T(8,128)(2,1)S(1)}, bf16[128,512]{1,0:T(8,128)(2,1)S(1)}, u32[]{:S(2)}, u32[]{:S(2)}) %collective-permute-start.103) | collective-permute-done | bytes 131104 | tf_op jit(solution)/shard_map/ppermute | solution.py:26
  243.4 4.2 collective-permute-done.109
  247.6 4.2 collective-permute-done.104
  268.3 3.9 multiply_reduce_fusion.5
  288.4 5.1 fusion.22
  306.3 3.6 fusion.41
  344.2 4.1 collective-permute-start.88
  355.2 3.6 collective-permute-done.89
  358.9 3.7 collective-permute-done.84
  363.5 4.7 collective-permute-done.76
  369.9 4.0 collective-permute-done.71
  403.7 4.3 collective-permute-done.42
  421.8 6.8 %collective-permute-done.98 = bf16[128,1024]{1,0:T(8,128)(2,1)} collective-permute-done((bf16[128,1024]{1,0:T(8,128)(2,1)}, bf16[128,1024]{1,0:T(8,128)(2,1)}, u32[]{:S(2)}, u32[]{:S(2)}) %collective-permute-start.98) | collective-permute-done | bytes 262176 | tf_op jit(solution)/shard_map/ppermute | solution.py:26
  436.2 4.0 collective-permute-done.77
  441.2 4.0 collective-permute-done.99
  445.8 4.3 collective-permute-done.94
  451.9 3.9 collective-permute-done.72
  463.9 6.0 %collective-permute-done.78 = bf16[128,384]{1,0:T(8,128)(2,1)S(1)} collective-permute-done((bf16[128,384]{1,0:T(8,128)(2,1)}, bf16[128,384]{1,0:T(8,128)(2,1)S(1)}, u32[]{:S(2)}, u32[]{:S(2)}) %collective-permute-start.78) | collective-permute-done | bytes 98336 | tf_op jit(solution)/shard_map/ppermute | solution.py:26
  470.8 4.8 collective-permute-done.73
  477.8 4.4 collective-permute-done.51
  485.3 4.2 collective-permute-done.79
  489.5 4.5 collective-permute-done.74
  494.2 6.3 %collective-permute-done.52 = bf16[128,512]{1,0:T(8,128)(2,1)S(1)} collective-permute-done((bf16[128,512]{1,0:T(8,128)(2,1)S(1)}, bf16[128,512]{1,0:T(8,128)(2,1)S(1)}, u32[]{:S(2)}, u32[]{:S(2)}) %collective-permute-start.52) | collective-permute-done | bytes 131104 | tf_op jit(solution)/shard_map/ppermute | solution.py:26
  501.4 4.3 collective-permute-done.53
  516.2 7.7 %collective-permute-done.62 = bf16[128,512]{1,0:T(8,128)(2,1)S(1)} collective-permute-done((bf16[128,512]{1,0:T(8,128)(2,1)S(1)}, bf16[128,512]{1,0:T(8,128)(2,1)S(1)}, u32[]{:S(2)}, u32[]{:S(2)}) %collective-permute-start.62) | collective-permute-done | bytes 131104 | tf_op jit(solution)/shard_map/ppermute | solution.py:26
  (966 shorter events, 375.5 us)
Async XLA Ops:
  6.2 32.7 %collective-permute-start.16 = (bf16[128,1152]{1,0:T(8,128)(2,1)}, bf16[128,1152]{1,0:T(8,128)(2,1)}, u32[]{:S(2)}, u32[]{:S(2)}) collective-permute-start(bf16[128,1152]{1,0:T(8,128)(2,1)} %get-tuple-element.253), channel_id=1, source_target_pairs={{0,8},{8,0},{16,24},{24,16},{1,9},{9,1},{17,25},{25,17},{2,10},{10... | collective-permute-start | bytes 884744 | tf_op jit(solution)/shard_map/ppermute | solution.py:26
  9.1 35.4 %collective-permute-start.18 = (bf16[128,1152]{1,0:T(8,128)(2,1)}, bf16[128,1152]{1,0:T(8,128)(2,1)}, u32[]{:S(2)}, u32[]{:S(2)}) collective-permute-start(bf16[128,1152]{1,0:T(8,128)(2,1)} %get-tuple-element.253), channel_id=1, source_target_pairs={{0,16},{8,24},{16,0},{24,8},{1,17},{9,25},{17,1},{25,9},{2,18},{10... | collective-permute-start | bytes 884744 | tf_op jit(solution)/shard_map/ppermute | solution.py:26
  12.0 22.4 %collective-permute-start.11 = (bf16[128,1024]{0,1:T(8,128)(2,1)}, bf16[128,1024]{0,1:T(8,128)(2,1)}, u32[]{:S(2)}, u32[]{:S(2)}) collective-permute-start(bf16[128,1024]{0,1:T(8,128)(2,1)} %get-tuple-element.269), channel_id=1, source_target_pairs={{0,16},{8,24},{16,0},{24,8},{1,17},{9,25},{17,1},{25,9},{2,18},{10... | collective-permute-start | bytes 786440 | tf_op jit(solution)/shard_map/ppermute | solution.py:26
  46.2 89.2 %collective-permute-start.28 = (bf16[128,3072]{1,0:T(8,128)(2,1)}, bf16[128,3072]{1,0:T(8,128)(2,1)}, u32[]{:S(2)}, u32[]{:S(2)}) collective-permute-start(bf16[128,3072]{1,0:T(8,128)(2,1)} %get-tuple-element.238), channel_id=1, source_target_pairs={{0,8},{8,0},{16,24},{24,16},{1,9},{9,1},{17,25},{25,17},{2,10},{10... | collective-permute-start | bytes 2359304 | tf_op jit(solution)/shard_map/ppermute | solution.py:26
  48.5 93.1 %collective-permute-start.30 = (bf16[128,3072]{1,0:T(8,128)(2,1)}, bf16[128,3072]{1,0:T(8,128)(2,1)}, u32[]{:S(2)}, u32[]{:S(2)}) collective-permute-start(bf16[128,3072]{1,0:T(8,128)(2,1)} %get-tuple-element.238), channel_id=1, source_target_pairs={{0,16},{8,24},{16,0},{24,8},{1,17},{9,25},{17,1},{25,9},{2,18},{10... | collective-permute-start | bytes 2359304 | tf_op jit(solution)/shard_map/ppermute | solution.py:26
  54.7 24.9 %collective-permute-start.13 = (bf16[128,1024]{0,1:T(8,128)(2,1)}, bf16[128,1024]{0,1:T(8,128)(2,1)S(1)}, u32[]{:S(2)}, u32[]{:S(2)}) collective-permute-start(bf16[128,1024]{0,1:T(8,128)(2,1)} %collective-permute-done.9), channel_id=1, source_target_pairs={{0,16},{8,24},{16,0},{24,8},{1,17},{9,25},{17,1},{25,9},{2,18},{10... | collective-permute-start | bytes 786440 | tf_op jit(solution)/shard_map/ppermute | solution.py:26
  55.8 26.1 %collective-permute-start.14 = (bf16[128,1024]{0,1:T(8,128)(2,1)S(1)}, bf16[128,1024]{0,1:T(8,128)(2,1)S(1)}, u32[]{:S(2)}, u32[]{:S(2)}) collective-permute-start(bf16[128,1024]{0,1:T(8,128)(2,1)S(1)} %collective-permute-done.12), channel_id=1, source_target_pairs={{0,8},{8,0},{16,24},{24,16},{1,9},{9,1},{17,25},{25,17},{2,10},{10... | collective-permute-start | bytes 786440 | tf_op jit(solution)/shard_map/ppermute | solution.py:26
  57.3 28.7 %collective-permute-start.20 = (bf16[128,1152]{1,0:T(8,128)(2,1)}, bf16[128,1152]{1,0:T(8,128)(2,1)S(1)}, u32[]{:S(2)}, u32[]{:S(2)}) collective-permute-start(bf16[128,1152]{1,0:T(8,128)(2,1)} %collective-permute-done.16), channel_id=1, source_target_pairs={{0,16},{8,24},{16,0},{24,8},{1,17},{9,25},{17,1},{25,9},{2,18},{10... | collective-permute-start | bytes 884744 | tf_op jit(solution)/shard_map/ppermute | solution.py:26
  99.9 25.6 %collective-permute-start.8 = (bf16[256,128]{0,1:T(8,128)(2,1)}, bf16[256,128]{0,1:T(8,128)(2,1)}, u32[]{:S(2)}, u32[]{:S(2)}) collective-permute-start(bf16[256,128]{0,1:T(8,128)(2,1)} %bitcast.12), channel_id=1, source_target_pairs={{0,6},{1,7},{8,14},{9,15},{16,22},{17,23},{24,30},{25,31}} | collective-permute-start | bytes 196616 | tf_op jit(solution)/shard_map/ppermute | solution.py:22
  106.0 21.4 %collective-permute-start.7 = (bf16[256,128]{0,1:T(8,128)(2,1)}, bf16[256,128]{0,1:T(8,128)(2,1)}, u32[]{:S(2)}, u32[]{:S(2)}) collective-permute-start(bf16[256,128]{0,1:T(8,128)(2,1)} %bitcast.12), channel_id=1, source_target_pairs={{0,4},{2,6},{1,5},{3,7},{8,12},{10,14},{9,13},{11,15},{16,20},{18,... | collective-permute-start | bytes 196616 | tf_op jit(solution)/shard_map/ppermute | solution.py:22
  141.6 26.6 %collective-permute-start.15 = (f32[256,1024]{1,0:T(8,128)}, f32[256,1024]{1,0:T(8,128)}, u32[]{:S(2)}, u32[]{:S(2)}) collective-permute-start(f32[256,1024]{1,0:T(8,128)} %fusion.102), channel_id=1, source_target_pairs={{0,1},{1,0},{2,3},{3,2},{4,5},{5,4},{6,7},{7,6},{8,9},{9,8},{10,11... | collective-permute-start | bytes 3145736 | tf_op jit(solution)/shard_map/ppermute | solution.py:26
  145.4 20.8 %collective-permute-start.33 = (bf16[128,3072]{1,0:T(8,128)(2,1)}, bf16[128,3072]{1,0:T(8,128)(2,1)}, u32[]{:S(2)}, u32[]{:S(2)}) collective-permute-start(bf16[128,3072]{1,0:T(8,128)(2,1)} %collective-permute-done.31), channel_id=1, source_target_pairs={{0,8},{8,0},{16,24},{24,16},{1,9},{9,1},{17,25},{25,17},{2,10},{10... | collective-permute-start | bytes 2359304 | tf_op jit(solution)/shard_map/ppermute | solution.py:26
  193.0 60.9 %collective-permute-start.35 = (f32[256,1024]{1,0:T(8,128)S(1)}, f32[256,1024]{1,0:T(8,128)S(1)}, u32[]{:S(2)}, u32[]{:S(2)}) collective-permute-start(f32[256,1024]{1,0:T(8,128)S(1)} %fusion.3), channel_id=1, source_target_pairs={{0,1},{1,0},{2,3},{3,2},{4,5},{5,4},{6,7},{7,6},{8,9},{9,8},{10,11... | collective-permute-start | bytes 3145736 | tf_op jit(solution)/shard_map/ppermute | solution.py:26
  193.1 63.5 %collective-permute-start.34 = (f32[256,1024]{1,0:T(8,128)S(1)}, f32[256,1024]{1,0:T(8,128)S(1)}, u32[]{:S(2)}, u32[]{:S(2)}) collective-permute-start(f32[256,1024]{1,0:T(8,128)S(1)} %fusion.19), channel_id=1, source_target_pairs={{0,1},{1,0},{2,3},{3,2},{4,5},{5,4},{6,7},{7,6},{8,9},{9,8},{10,11... | collective-permute-start | bytes 3145736 | tf_op jit(solution)/shard_map/ppermute | solution.py:26
  193.6 21.8 %collective-permute-start.96 = (bf16[256,1024]{1,0:T(8,128)(2,1)S(1)}, bf16[256,1024]{1,0:T(8,128)(2,1)S(1)}, u32[]{:S(2)}, u32[]{:S(2)}) collective-permute-start(bf16[256,1024]{1,0:T(8,128)(2,1)S(1)} %convolution_convert_fusion), channel_id=1, source_target_pairs={{0,16},{8,24},{16,0},{24,8},{1,17},{9,25},{17,1},{25,9},{2,18},{10... | collective-permute-start | bytes 1572872 | tf_op jit(solution)/shard_map/ppermute | solution.py:26
  203.9 105.9 %collective-permute-start.95 = (bf16[256,1024]{1,0:T(8,128)(2,1)}, bf16[256,1024]{1,0:T(8,128)(2,1)}, u32[]{:S(2)}, u32[]{:S(2)}) collective-permute-start(bf16[256,1024]{1,0:T(8,128)(2,1)} %convolution_convert_fusion.1), channel_id=1, source_target_pairs={{0,16},{8,24},{16,0},{24,8},{1,17},{9,25},{17,1},{25,9},{2,18},{10... | collective-permute-start | bytes 1572872 | tf_op jit(solution)/shard_map/ppermute | solution.py:26
  215.4 99.5 %collective-permute-start.90 = (bf16[256,1024]{1,0:T(8,128)(2,1)}, bf16[256,1024]{1,0:T(8,128)(2,1)}, u32[]{:S(2)}, u32[]{:S(2)}) collective-permute-start(bf16[256,1024]{1,0:T(8,128)(2,1)} %convolution_convert_fusion.3), channel_id=1, source_target_pairs={{0,8},{8,0},{16,24},{24,16},{1,9},{9,1},{17,25},{25,17},{2,10},{10... | collective-permute-start | bytes 1572872 | tf_op jit(solution)/shard_map/ppermute | solution.py:26
  251.9 59.4 %collective-permute-start.97 = (bf16[256,1024]{1,0:T(8,128)(2,1)}, bf16[256,1024]{1,0:T(8,128)(2,1)}, u32[]{:S(2)}, u32[]{:S(2)}) collective-permute-start(bf16[256,1024]{1,0:T(8,128)(2,1)} %add_convert_fusion), channel_id=1, source_target_pairs={{0,8},{8,0},{16,24},{24,16},{1,9},{9,1},{17,25},{25,17},{2,10},{10... | collective-permute-start | bytes 1572872 | tf_op jit(solution)/shard_map/ppermute | solution.py:26
  253.8 62.3 %collective-permute-start.92 = (bf16[256,1024]{1,0:T(8,128)(2,1)}, bf16[256,1024]{1,0:T(8,128)(2,1)}, u32[]{:S(2)}, u32[]{:S(2)}) collective-permute-start(bf16[256,1024]{1,0:T(8,128)(2,1)} %add_convert_fusion.1), channel_id=1, source_target_pairs={{0,16},{8,24},{16,0},{24,8},{1,17},{9,25},{17,1},{25,9},{2,18},{10... | collective-permute-start | bytes 1572872 | tf_op jit(solution)/shard_map/ppermute | solution.py:26
  295.5 84.6 %collective-permute-start.41 = (bf16[784,128]{1,0:T(8,128)(2,1)}, bf16[784,128]{1,0:T(8,128)(2,1)}, u32[]{:S(2)}, u32[]{:S(2)}) collective-permute-start(bf16[784,128]{1,0:T(8,128)(2,1)} %pad_maximum_fusion.11), channel_id=1, source_target_pairs={{6,0},{7,1},{14,8},{15,9},{22,16},{23,17},{30,24},{31,25}} | collective-permute-start | bytes 602120 | tf_op jit(solution)/shard_map/ppermute | solution.py:22
  309.9 65.7 %collective-permute-start.39 = (bf16[784,128]{1,0:T(8,128)(2,1)}, bf16[784,128]{1,0:T(8,128)(2,1)}, u32[]{:S(2)}, u32[]{:S(2)}) collective-permute-start(bf16[784,128]{1,0:T(8,128)(2,1)} %pad_maximum_fusion.11), channel_id=1, source_target_pairs={{2,0},{4,2},{6,4},{3,1},{5,3},{7,5},{10,8},{12,10},{14,12},{11,9},... | collective-permute-start | bytes 602120 | tf_op jit(solution)/shard_map/ppermute | solution.py:22
  323.0 54.0 %collective-permute-start.40 = (bf16[784,128]{1,0:T(8,128)(2,1)}, bf16[784,128]{1,0:T(8,128)(2,1)}, u32[]{:S(2)}, u32[]{:S(2)}) collective-permute-start(bf16[784,128]{1,0:T(8,128)(2,1)} %pad_maximum_fusion.11), channel_id=1, source_target_pairs={{4,0},{6,2},{5,1},{7,3},{12,8},{14,10},{13,9},{15,11},{20,16},{22,... | collective-permute-start | bytes 602120 | tf_op jit(solution)/shard_map/ppermute | solution.py:22
  341.9 77.9 %collective-permute-start.50 = (bf16[256,512]{1,0:T(8,128)(2,1)}, bf16[256,512]{1,0:T(8,128)(2,1)}, u32[]{:S(2)}, u32[]{:S(2)}) collective-permute-start(bf16[256,512]{1,0:T(8,128)(2,1)} %convolution_convert_fusion.14), channel_id=1, source_target_pairs={{0,8},{8,0},{16,24},{24,16},{1,9},{9,1},{17,25},{25,17},{2,10},{10... | collective-permute-start | bytes 786440 | tf_op jit(solution)/shard_map/ppermute | solution.py:26
  373.9 102.9 %collective-permute-start.49 = (bf16[256,512]{1,0:T(8,128)(2,1)}, bf16[256,512]{1,0:T(8,128)(2,1)}, u32[]{:S(2)}, u32[]{:S(2)}) collective-permute-start(bf16[256,512]{1,0:T(8,128)(2,1)} %convolution_convert_fusion.15), channel_id=1, source_target_pairs={{0,8},{8,0},{16,24},{24,16},{1,9},{9,1},{17,25},{25,17},{2,10},{10... | collective-permute-start | bytes 786440 | tf_op jit(solution)/shard_map/ppermute | solution.py:26
  375.6 58.9 %collective-permute-start.75 = (bf16[256,384]{1,0:T(8,128)(2,1)}, bf16[256,384]{1,0:T(8,128)(2,1)}, u32[]{:S(2)}, u32[]{:S(2)}) collective-permute-start(bf16[256,384]{1,0:T(8,128)(2,1)} %convolution_convert_fusion.17), channel_id=1, source_target_pairs={{0,16},{8,24},{16,0},{24,8},{1,17},{9,25},{17,1},{25,9},{2,18},{10... | collective-permute-start | bytes 589832 | tf_op jit(solution)/shard_map/ppermute | solution.py:26
  377.1 74.8 %collective-permute-start.70 = (bf16[256,384]{1,0:T(8,128)(2,1)}, bf16[256,384]{1,0:T(8,128)(2,1)}, u32[]{:S(2)}, u32[]{:S(2)}) collective-permute-start(bf16[256,384]{1,0:T(8,128)(2,1)} %convolution_convert_fusion.19), channel_id=1, source_target_pairs={{0,8},{8,0},{16,24},{24,16},{1,9},{9,1},{17,25},{25,17},{2,10},{10... | collective-permute-start | bytes 589832 | tf_op jit(solution)/shard_map/ppermute | solution.py:26
  428.6 30.8 %collective-permute-start.55 = (bf16[256,640]{1,0:T(8,128)(2,1)}, bf16[256,640]{1,0:T(8,128)(2,1)}, u32[]{:S(2)}, u32[]{:S(2)}) collective-permute-start(bf16[256,640]{1,0:T(8,128)(2,1)} %convolution_convert_fusion.6), channel_id=1, source_target_pairs={{0,16},{8,24},{16,0},{24,8},{1,17},{9,25},{17,1},{25,9},{2,18},{10... | collective-permute-start | bytes 983048 | tf_op jit(solution)/shard_map/ppermute | solution.py:26
  434.5 71.7 %collective-permute-start.54 = (bf16[256,640]{1,0:T(8,128)(2,1)S(1)}, bf16[256,640]{1,0:T(8,128)(2,1)}, u32[]{:S(2)}, u32[]{:S(2)}) collective-permute-start(bf16[256,640]{1,0:T(8,128)(2,1)S(1)} %copy-done.96), channel_id=1, source_target_pairs={{0,16},{8,24},{16,0},{24,8},{1,17},{9,25},{17,1},{25,9},{2,18},{10... | collective-permute-start | bytes 983048 | tf_op jit(solution)/shard_map/ppermute | solution.py:26
  451.8 86.0 %collective-permute-start.43 = (f32[256,1024]{1,0:T(8,128)S(1)}, f32[256,1024]{1,0:T(8,128)}, u32[]{:S(2)}, u32[]{:S(2)}) collective-permute-start(f32[256,1024]{1,0:T(8,128)S(1)} %convolution_add_fusion), channel_id=1, source_target_pairs={{0,1},{1,0},{2,3},{3,2},{4,5},{5,4},{6,7},{7,6},{8,9},{9,8},{10,11... | collective-permute-start | bytes 3145736 | tf_op jit(solution)/shard_map/ppermute | solution.py:26
  459.5 25.4 %collective-permute-start.65 = (bf16[256,640]{1,0:T(8,128)(2,1)}, bf16[256,640]{1,0:T(8,128)(2,1)S(1)}, u32[]{:S(2)}, u32[]{:S(2)}) collective-permute-start(bf16[256,640]{1,0:T(8,128)(2,1)} %convolution_convert_fusion.4), channel_id=1, source_target_pairs={{0,16},{8,24},{16,0},{24,8},{1,17},{9,25},{17,1},{25,9},{2,18},{10... | collective-permute-start | bytes 983048 | tf_op jit(solution)/shard_map/ppermute | solution.py:26
  476.8 38.5 %collective-permute-start.64 = (bf16[256,640]{1,0:T(8,128)(2,1)S(1)}, bf16[256,640]{1,0:T(8,128)(2,1)S(1)}, u32[]{:S(2)}, u32[]{:S(2)}) collective-permute-start(bf16[256,640]{1,0:T(8,128)(2,1)S(1)} %copy-done.97), channel_id=1, source_target_pairs={{0,16},{8,24},{16,0},{24,8},{1,17},{9,25},{17,1},{25,9},{2,18},{10... | collective-permute-start | bytes 983048 | tf_op jit(solution)/shard_map/ppermute | solution.py:26
  482.1 25.5 %collective-permute-start.56 = (bf16[256,640]{1,0:T(8,128)(2,1)S(1)}, bf16[256,640]{1,0:T(8,128)(2,1)S(1)}, u32[]{:S(2)}, u32[]{:S(2)}) collective-permute-start(bf16[256,640]{1,0:T(8,128)(2,1)S(1)} %add_convert_fusion.4), channel_id=1, source_target_pairs={{0,8},{8,0},{16,24},{24,16},{1,9},{9,1},{17,25},{25,17},{2,10},{10... | collective-permute-start | bytes 983048 | tf_op jit(solution)/shard_map/ppermute | solution.py:26
  (281 other events, 2647.6 us)
